TPU v7x, 32 devices: a whole 2x2x4 slice. The times are simulated.
32 devices in a mesh: slab: 2 (over x), tm: 16 (over z, y, core), band: 1.
Axes of the slice: x: 2, y: 2, z: 4, core: 2. Of those that a mesh axis runs over, the one named last changes fastest.
Arguments:
- tokens: bfloat16 [64, 4, 128, 1024], P(('slab', 'tm'), 'band'), parts along dimension 0
- norm_gain: float32 [1024], replicated, may hold values from 0.1 to 1.9
- query_weight: bfloat16 [1024, 1024], replicated
- key_weight: bfloat16 [1024, 1024], replicated
- value_weight: bfloat16 [1024, 1024], replicated, may hold values from -0.1875 to 0.1875
- out_weight: bfloat16 [1024, 1024], replicated, may hold values from -3 to 3
- key_frames: int32 [4], P('slab'), parts along dimension 0, may hold values from 0 to 31, as said below
Outputs:
- updated: bfloat16 [64, 4, 128, 1024], P(('slab', 'tm'), 'band'), parts along dimension 0
There are 2 independent parts, one for each index of `slab`. A program takes and returns all parts, laid end to end along the dimension named above; an argument that names none is the same for every part. Nothing has to cross between parts.
Inputs may be any that keep to these rules, and one draw needn't show every extreme that they name: key_frames[k] is 16 * k plus an offset of 0 to 15; the first keyframe is frame 0 and the last is frame 32 - 1.
All inputs are finite; a program needn't handle non-finite values.
Results may differ from a plain program's by a relative error of at most 0.0061.
Values may be sent and summed in bfloat16 or wider, within the bound.
A program may use at most 192 MiB of HBM per device.

v0:
```python
import jax
import jax.numpy as jnp
from jax import lax
from jax.sharding import PartitionSpec as P

HEAD_DIM = 64
FRAME_REACH = 2
BAND_REACH = 1


def padded(cells, sides, width):
    for axis, dim in sides:
        count = lax.axis_size(axis)
        ends = count - 1
        head = lax.slice_in_dim(cells, 0, width, axis=dim)
        tail = lax.slice_in_dim(cells, cells.shape[dim] - width, cells.shape[dim], axis=dim)
        cells = jnp.concatenate(
            [
                lax.ppermute(tail, axis, [(i, (i + 1) % count) for i in range(ends)]),
                cells,
                lax.ppermute(head, axis, [((i + 1) % count, i) for i in range(ends)]),
            ],
            axis=dim,
        )
    return cells


def from_root(array, axis, root):
    mine = lax.axis_index(axis) == root
    return lax.psum(jnp.where(mine, array, jnp.zeros_like(array)), axis)


def layer_norm(token_rows, norm_gain):
    rows_float = token_rows.astype(jnp.float32)
    centred = rows_float - jnp.mean(rows_float, axis=-1, keepdims=True)
    variance = jnp.mean(centred * centred, axis=-1, keepdims=True)
    return (centred * lax.rsqrt(variance + 1e-05) * norm_gain).astype(jnp.bfloat16)


def attend(queries, key_values, allowed, width_model):
    head_count = width_model // HEAD_DIM
    query_heads = queries.reshape(queries.shape[0], head_count, HEAD_DIM)
    key_heads = key_values[:, :width_model].reshape(-1, head_count, HEAD_DIM)
    value_heads = key_values[:, width_model:].reshape(-1, head_count, HEAD_DIM)
    scores = jnp.einsum(
        "qhd,khd->hqk", query_heads, key_heads, preferred_element_type=jnp.float32
    ) * HEAD_DIM ** (-0.5)
    scores = jnp.where(allowed[None, None, :], scores, jnp.float32(-1e30))
    largest = jnp.max(scores, axis=-1, keepdims=True)
    weights = jnp.exp(scores - largest)
    denominator = jnp.sum(weights, axis=-1)
    probs = weights.astype(jnp.bfloat16)
    context = jnp.einsum("hqk,khd->qhd", probs, value_heads, preferred_element_type=jnp.float32)
    context = context / jnp.transpose(denominator)[:, :, None]
    return context.reshape(queries.shape[0], width_model).astype(jnp.bfloat16)


def per_device(tokens, norm_gain, query_weight, key_weight, value_weight, out_weight, key_frames):
    frame_count, band_count, band_tokens, width_model = tokens.shape
    token_rows = tokens.reshape(-1, width_model)
    normed = layer_norm(token_rows, norm_gain)
    queries = jnp.dot(normed, query_weight, preferred_element_type=jnp.float32).astype(jnp.bfloat16)
    key_rows = jnp.dot(normed, key_weight, preferred_element_type=jnp.float32).astype(jnp.bfloat16)
    values = jnp.dot(normed, value_weight, preferred_element_type=jnp.float32).astype(jnp.bfloat16)
    queries = queries.reshape(frame_count, band_count, band_tokens, width_model)
    key_value = jnp.concatenate([key_rows, values], axis=1).reshape(
        frame_count, band_count, band_tokens, 2 * width_model
    )
    banded = padded(key_value, (("band", 1),), BAND_REACH)
    extended = padded(banded, (("tm", 0),), FRAME_REACH)
    first_frame = lax.axis_index("tm") * frame_count
    first_band = lax.axis_index("band") * band_count
    frames_total = lax.axis_size("tm") * frame_count
    bands_total = lax.axis_size("band") * band_count
    keyframe_count = key_frames.shape[0]

    def fetch(number, store):
        target = key_frames[number]
        owner = target // frame_count
        local = jnp.clip(target - first_frame, 0, frame_count - 1)
        candidate = lax.dynamic_index_in_dim(key_value, local, 0, keepdims=False)
        arrived = from_root(candidate, "tm", owner)
        return lax.dynamic_update_index_in_dim(store, arrived, number, 0)

    empty = jnp.zeros((keyframe_count, band_count, band_tokens, 2 * width_model), jnp.bfloat16)
    keyframe_store = lax.fori_loop(0, keyframe_count, fetch, empty)
    frame_span = 2 * FRAME_REACH + 1
    band_span = 2 * BAND_REACH + 1

    def one_block(number):
        frame_local = number // band_count
        band_local = number % band_count
        window = lax.dynamic_slice(
            extended,
            (frame_local, band_local, 0, 0),
            (frame_span, band_span, band_tokens, 2 * width_model),
        )
        frame_now = first_frame + frame_local
        band_now = first_band + band_local
        window_frame = frame_now - FRAME_REACH + jnp.arange(frame_span, dtype=jnp.int32)
        window_band = band_now - BAND_REACH + jnp.arange(band_span, dtype=jnp.int32)
        frame_valid = (window_frame >= 0) & (window_frame < frames_total)
        band_valid = (window_band >= 0) & (window_band < bands_total)
        allowed_window = jnp.broadcast_to(
            (frame_valid[:, None] & band_valid[None, :])[:, :, None],
            (frame_span, band_span, band_tokens),
        ).reshape(-1)
        allowed_keyframe = jnp.broadcast_to(
            (jnp.abs(frame_now - key_frames) > FRAME_REACH)[:, None], (keyframe_count, band_tokens)
        ).reshape(-1)
        allowed = jnp.concatenate([allowed_window, allowed_keyframe], axis=0)
        keyframe_band = lax.dynamic_index_in_dim(keyframe_store, band_local, 1, keepdims=False)
        key_values = jnp.concatenate(
            [window.reshape(-1, 2 * width_model), keyframe_band.reshape(-1, 2 * width_model)],
            axis=0,
        )
        block_queries = lax.dynamic_index_in_dim(
            lax.dynamic_index_in_dim(queries, frame_local, 0, keepdims=False),
            band_local,
            0,
            keepdims=False,
        )
        return attend(block_queries, key_values, allowed, width_model)

    context = lax.map(one_block, jnp.arange(frame_count * band_count, dtype=jnp.int32)).reshape(
        -1, width_model
    )
    updated = token_rows.astype(jnp.float32) + jnp.dot(
        context, out_weight, preferred_element_type=jnp.float32
    )
    return updated.astype(jnp.bfloat16).reshape(frame_count, band_count, band_tokens, width_model)


def solution(mesh):
    in_specs = (P(("slab", "tm"), "band", None, None), P(), P(), P(), P(), P(), P("slab"))
    out_specs = P(("slab", "tm"), "band", None, None)
    return jax.shard_map(
        per_device, mesh=mesh, in_specs=in_specs, out_specs=out_specs, check_vma=False
    )
```

profile of v0, /device:TPU:6, one launch (start us, length us, event | category | flops | bytes accessed | tf_op | source)
XLA Modules:
  0.0 990.2 jit_solution(12884060559468418726)
XLA Ops:
  18.9 6.5 copy.20
  45.2 128.4 %collective-permute-done.2 = bf16[2,6,128,2048]{3,2,1,0:T(8,128)(2,1)} collective-permute-done((bf16[2,6,128,2048]{3,2,1,0:T(8,128)(2,1)}, bf16[2,6,128,2048]{3,2,1,0:T(8,128)(2,1)}, u32[]{:S(2)}, u32[]{:S(2)}) %collective-permute-start.2) | collective-permute-done | bytes 6291488 | tf_op jit(solution)/shard_map/ppermute | solution.py:19
  173.6 12.8 %pad_maximum_fusion.1 = bf16[6,6,128,2048]{3,2,1,0:T(8,128)(2,1)} fusion(bf16[2,6,128,2048]{3,2,1,0:T(8,128)(2,1)} %collective-permute-done.3, bf16[2,1,128,2048]{3,2,1,0:T(8,128)(2,1)S(1)} %collective-permute-done.1, bf16[2,4,128,2048]{3,2,1,0:T(8,128)(2,1)S(1)} %bitcast.80, bf16[2,1,128,2048]{3,2,1,0:T(8,128)(2,1)S(1)} %collective-permute-done, ...), kind=kLoop, calls=%fused_computation.28 | loop fusion | flops 37748736 | bytes 37748736 | tf_op jit(solution)/shard_map/concatenate | solution.py:17
  186.4 215.8 %while.28 = (s32[]{:T(128)}, bf16[2,4,128,2048]{3,2,1,0:T(8,128)(2,1)}, s32[2]{0:T(128)S(1)}, s32[]{:T(128)}, bf16[2,4,128,2048]{3,2,1,0:T(8,128)(2,1)}, /*index=5*/s32[]{:T(128)}, s32[]{:T(128)}, u32[]{:T(128)}, s32[]{:T(128)}) while((s32[]{:T(128)}, bf16[2,4,128,2048]{3,2,1,0:T(8,128)(2,1)}, s32[2]{0:T(128)S(1)}, s32[]{:T(128)}, ...), condition=%wide.region_4.5_spmd, body=%wide.region_2.4_spmd.sunk | while | flops 2097175 | bytes 20971896 | solution.py:86
  193.4 98.4 %all-reduce.2.cloned.1.call-done = bf16[1,4,128,2048]{3,2,1,0:T(8,128)(2,1)} async-done(((bf16[1,4,128,2048]{3,2,1,0:T(8,128)(2,1)}), bf16[1,4,128,2048]{3,2,1,0:T(8,128)(2,1)}) %all-reduce.2.cloned.1.call-update) | async-done | bytes 2097168 | tf_op jit(solution)/shard_map/while/body/eval_jaxpr/psum | solution.py:30
  301.9 97.2 %all-reduce.2.cloned.1.call-done = bf16[1,4,128,2048]{3,2,1,0:T(8,128)(2,1)} async-done(((bf16[1,4,128,2048]{3,2,1,0:T(8,128)(2,1)}), bf16[1,4,128,2048]{3,2,1,0:T(8,128)(2,1)}) %all-reduce.2.cloned.1.call-update) | async-done | bytes 2097168 | tf_op jit(solution)/shard_map/while/body/eval_jaxpr/psum | solution.py:30
  402.2 574.5 %while.29 = (s32[]{:T(128)}, bf16[8,128,1024]{2,1,0:T(8,128)(2,1)}, s32[8]{0:T(128)S(1)}, bf16[6,6,128,2048]{3,2,1,0:T(8,128)(2,1)}, bf16[2,4,128,2048]{3,2,1,0:...) while((s32[]{:T(128)}, bf16[8,128,1024]{2,1,0:T(8,128)(2,1)}, ...), condition=%wide.region_8.9_spmd, body=%wide.region_5.8_spmd.sunk | while | flops 1207957760 | bytes 118548080 | solution.py:125
  405.4 8.0 constant_dynamic-slice_fusion.7
  414.7 11.7 %pad_maximum_fusion.5 = (bf16[2176,1024]{1,0:T(8,128)(2,1)}, bf16[2176,1024]{1,0:T(8,128)(2,1)}) fusion(bf16[256,2048]{1,0:T(8,128)(2,1)S(1)} %bitcast.82, bf16[1920,2048]{1,0:T(8,128)(2,1)} %bitcast.76), kind=kLoop, calls=%fused_computation.12.clone.1 | loop fusion | flops 17825792 | bytes 17825792 | tf_op jit(solution)/shard_map/while/body/eval_jaxpr/concatenate | solution.py:113
  426.4 6.5 copy.31
  434.4 10.9 %fusion.47 = (f32[16,128]{1,0:T(8,128)S(1)}, f32[16,128,2176]{2,1,0:T(8,128)}) fusion(pred[2176]{0:T(1024)(128)(4,1)S(1)} %pad_add_fusion.2, bf16[128,16,64]{0,2,1:T(8,128)(2,1)S(1)} %bitcast.83, bf16[2176,16,64]{0,2,1:T(8,128)(2,1)} %bitcast.75), kind=kOutput, calls=%fused_computation.4.clone.1 | convolution fusion | flops 583792640 | bytes 22554752 | tf_op jit(solution)/shard_map/while/body/eval_jaxpr/qhd,khd->hqk/dot_general | solution.py:45
  445.3 9.7 fusion.48
  455.0 6.5 copy.29
  461.6 11.6 %fusion.49 = bf16[128,16,64]{0,2,1:T(8,128)(2,1)S(1)} fusion(bf16[2176,16,64]{0,2,1:T(8,128)(2,1)} %bitcast.81, f32[16,128,2176]{2,1,0:T(8,128)} %get-tuple-element.433, f32[16,128]{1,0:T(8,128)S(1)} %get-tuple-element.434, pred[2176]{0:T(1024)(128)(4,1)S(1)} %pad_add_fusion.2, f32[128,16]{0,1:T(8,128)S(1)} %bitcast.86), kind=kOutput, calls=%fused_computation.15.clone.1 | convolution fusion | flops 588513280 | bytes 22562944 | tf_op jit(solution)/shard_map/while/body/eval_jaxpr/hqk,khd->qhd/dot_general | solution.py:53
  477.3 8.0 constant_dynamic-slice_fusion.7
  486.5 11.7 %pad_maximum_fusion.5 = (bf16[2176,1024]{1,0:T(8,128)(2,1)}, bf16[2176,1024]{1,0:T(8,128)(2,1)}) fusion(bf16[256,2048]{1,0:T(8,128)(2,1)S(1)} %bitcast.82, bf16[1920,2048]{1,0:T(8,128)(2,1)} %bitcast.76), kind=kLoop, calls=%fused_computation.12.clone.1 | loop fusion | flops 17825792 | bytes 17825792 | tf_op jit(solution)/shard_map/while/body/eval_jaxpr/concatenate | solution.py:113
  498.2 6.5 copy.31
  506.2 10.9 %fusion.47 = (f32[16,128]{1,0:T(8,128)S(1)}, f32[16,128,2176]{2,1,0:T(8,128)}) fusion(pred[2176]{0:T(1024)(128)(4,1)S(1)} %pad_add_fusion.2, bf16[128,16,64]{0,2,1:T(8,128)(2,1)S(1)} %bitcast.83, bf16[2176,16,64]{0,2,1:T(8,128)(2,1)} %bitcast.75), kind=kOutput, calls=%fused_computation.4.clone.1 | convolution fusion | flops 583792640 | bytes 22554752 | tf_op jit(solution)/shard_map/while/body/eval_jaxpr/qhd,khd->hqk/dot_general | solution.py:45
  517.1 9.7 fusion.48
  526.8 6.5 copy.29
  533.4 11.6 %fusion.49 = bf16[128,16,64]{0,2,1:T(8,128)(2,1)S(1)} fusion(bf16[2176,16,64]{0,2,1:T(8,128)(2,1)} %bitcast.81, f32[16,128,2176]{2,1,0:T(8,128)} %get-tuple-element.433, f32[16,128]{1,0:T(8,128)S(1)} %get-tuple-element.434, pred[2176]{0:T(1024)(128)(4,1)S(1)} %pad_add_fusion.2, f32[128,16]{0,1:T(8,128)S(1)} %bitcast.86), kind=kOutput, calls=%fused_computation.15.clone.1 | convolution fusion | flops 588513280 | bytes 22562944 | tf_op jit(solution)/shard_map/while/body/eval_jaxpr/hqk,khd->qhd/dot_general | solution.py:53
  549.1 8.0 constant_dynamic-slice_fusion.7
  558.3 11.7 %pad_maximum_fusion.5 = (bf16[2176,1024]{1,0:T(8,128)(2,1)}, bf16[2176,1024]{1,0:T(8,128)(2,1)}) fusion(bf16[256,2048]{1,0:T(8,128)(2,1)S(1)} %bitcast.82, bf16[1920,2048]{1,0:T(8,128)(2,1)} %bitcast.76), kind=kLoop, calls=%fused_computation.12.clone.1 | loop fusion | flops 17825792 | bytes 17825792 | tf_op jit(solution)/shard_map/while/body/eval_jaxpr/concatenate | solution.py:113
  570.0 6.5 copy.31
  578.0 10.9 %fusion.47 = (f32[16,128]{1,0:T(8,128)S(1)}, f32[16,128,2176]{2,1,0:T(8,128)}) fusion(pred[2176]{0:T(1024)(128)(4,1)S(1)} %pad_add_fusion.2, bf16[128,16,64]{0,2,1:T(8,128)(2,1)S(1)} %bitcast.83, bf16[2176,16,64]{0,2,1:T(8,128)(2,1)} %bitcast.75), kind=kOutput, calls=%fused_computation.4.clone.1 | convolution fusion | flops 583792640 | bytes 22554752 | tf_op jit(solution)/shard_map/while/body/eval_jaxpr/qhd,khd->hqk/dot_general | solution.py:45
  588.9 9.7 fusion.48
  598.6 6.5 copy.29
  605.2 11.6 %fusion.49 = bf16[128,16,64]{0,2,1:T(8,128)(2,1)S(1)} fusion(bf16[2176,16,64]{0,2,1:T(8,128)(2,1)} %bitcast.81, f32[16,128,2176]{2,1,0:T(8,128)} %get-tuple-element.433, f32[16,128]{1,0:T(8,128)S(1)} %get-tuple-element.434, pred[2176]{0:T(1024)(128)(4,1)S(1)} %pad_add_fusion.2, f32[128,16]{0,1:T(8,128)S(1)} %bitcast.86), kind=kOutput, calls=%fused_computation.15.clone.1 | convolution fusion | flops 588513280 | bytes 22562944 | tf_op jit(solution)/shard_map/while/body/eval_jaxpr/hqk,khd->qhd/dot_general | solution.py:53
  620.9 8.0 constant_dynamic-slice_fusion.7
  630.2 11.7 %pad_maximum_fusion.5 = (bf16[2176,1024]{1,0:T(8,128)(2,1)}, bf16[2176,1024]{1,0:T(8,128)(2,1)}) fusion(bf16[256,2048]{1,0:T(8,128)(2,1)S(1)} %bitcast.82, bf16[1920,2048]{1,0:T(8,128)(2,1)} %bitcast.76), kind=kLoop, calls=%fused_computation.12.clone.1 | loop fusion | flops 17825792 | bytes 17825792 | tf_op jit(solution)/shard_map/while/body/eval_jaxpr/concatenate | solution.py:113
  641.8 6.5 copy.31
  649.8 10.9 %fusion.47 = (f32[16,128]{1,0:T(8,128)S(1)}, f32[16,128,2176]{2,1,0:T(8,128)}) fusion(pred[2176]{0:T(1024)(128)(4,1)S(1)} %pad_add_fusion.2, bf16[128,16,64]{0,2,1:T(8,128)(2,1)S(1)} %bitcast.83, bf16[2176,16,64]{0,2,1:T(8,128)(2,1)} %bitcast.75), kind=kOutput, calls=%fused_computation.4.clone.1 | convolution fusion | flops 583792640 | bytes 22554752 | tf_op jit(solution)/shard_map/while/body/eval_jaxpr/qhd,khd->hqk/dot_general | solution.py:45
  660.7 9.7 fusion.48
  670.4 6.5 copy.29
  677.0 11.6 %fusion.49 = bf16[128,16,64]{0,2,1:T(8,128)(2,1)S(1)} fusion(bf16[2176,16,64]{0,2,1:T(8,128)(2,1)} %bitcast.81, f32[16,128,2176]{2,1,0:T(8,128)} %get-tuple-element.433, f32[16,128]{1,0:T(8,128)S(1)} %get-tuple-element.434, pred[2176]{0:T(1024)(128)(4,1)S(1)} %pad_add_fusion.2, f32[128,16]{0,1:T(8,128)S(1)} %bitcast.86), kind=kOutput, calls=%fused_computation.15.clone.1 | convolution fusion | flops 588513280 | bytes 22562944 | tf_op jit(solution)/shard_map/while/body/eval_jaxpr/hqk,khd->qhd/dot_general | solution.py:53
  692.7 8.0 constant_dynamic-slice_fusion.7
  702.0 11.7 %pad_maximum_fusion.5 = (bf16[2176,1024]{1,0:T(8,128)(2,1)}, bf16[2176,1024]{1,0:T(8,128)(2,1)}) fusion(bf16[256,2048]{1,0:T(8,128)(2,1)S(1)} %bitcast.82, bf16[1920,2048]{1,0:T(8,128)(2,1)} %bitcast.76), kind=kLoop, calls=%fused_computation.12.clone.1 | loop fusion | flops 17825792 | bytes 17825792 | tf_op jit(solution)/shard_map/while/body/eval_jaxpr/concatenate | solution.py:113
  713.6 6.5 copy.31
  721.6 10.9 %fusion.47 = (f32[16,128]{1,0:T(8,128)S(1)}, f32[16,128,2176]{2,1,0:T(8,128)}) fusion(pred[2176]{0:T(1024)(128)(4,1)S(1)} %pad_add_fusion.2, bf16[128,16,64]{0,2,1:T(8,128)(2,1)S(1)} %bitcast.83, bf16[2176,16,64]{0,2,1:T(8,128)(2,1)} %bitcast.75), kind=kOutput, calls=%fused_computation.4.clone.1 | convolution fusion | flops 583792640 | bytes 22554752 | tf_op jit(solution)/shard_map/while/body/eval_jaxpr/qhd,khd->hqk/dot_general | solution.py:45
  732.5 9.7 fusion.48
  742.3 6.5 copy.29
  748.8 11.6 %fusion.49 = bf16[128,16,64]{0,2,1:T(8,128)(2,1)S(1)} fusion(bf16[2176,16,64]{0,2,1:T(8,128)(2,1)} %bitcast.81, f32[16,128,2176]{2,1,0:T(8,128)} %get-tuple-element.433, f32[16,128]{1,0:T(8,128)S(1)} %get-tuple-element.434, pred[2176]{0:T(1024)(128)(4,1)S(1)} %pad_add_fusion.2, f32[128,16]{0,1:T(8,128)S(1)} %bitcast.86), kind=kOutput, calls=%fused_computation.15.clone.1 | convolution fusion | flops 588513280 | bytes 22562944 | tf_op jit(solution)/shard_map/while/body/eval_jaxpr/hqk,khd->qhd/dot_general | solution.py:53
  764.5 8.0 constant_dynamic-slice_fusion.7
  773.8 11.7 %pad_maximum_fusion.5 = (bf16[2176,1024]{1,0:T(8,128)(2,1)}, bf16[2176,1024]{1,0:T(8,128)(2,1)}) fusion(bf16[256,2048]{1,0:T(8,128)(2,1)S(1)} %bitcast.82, bf16[1920,2048]{1,0:T(8,128)(2,1)} %bitcast.76), kind=kLoop, calls=%fused_computation.12.clone.1 | loop fusion | flops 17825792 | bytes 17825792 | tf_op jit(solution)/shard_map/while/body/eval_jaxpr/concatenate | solution.py:113
  785.4 6.5 copy.31
  793.4 10.9 %fusion.47 = (f32[16,128]{1,0:T(8,128)S(1)}, f32[16,128,2176]{2,1,0:T(8,128)}) fusion(pred[2176]{0:T(1024)(128)(4,1)S(1)} %pad_add_fusion.2, bf16[128,16,64]{0,2,1:T(8,128)(2,1)S(1)} %bitcast.83, bf16[2176,16,64]{0,2,1:T(8,128)(2,1)} %bitcast.75), kind=kOutput, calls=%fused_computation.4.clone.1 | convolution fusion | flops 583792640 | bytes 22554752 | tf_op jit(solution)/shard_map/while/body/eval_jaxpr/qhd,khd->hqk/dot_general | solution.py:45
  804.3 9.7 fusion.48
  814.1 6.5 copy.29
  820.6 11.6 %fusion.49 = bf16[128,16,64]{0,2,1:T(8,128)(2,1)S(1)} fusion(bf16[2176,16,64]{0,2,1:T(8,128)(2,1)} %bitcast.81, f32[16,128,2176]{2,1,0:T(8,128)} %get-tuple-element.433, f32[16,128]{1,0:T(8,128)S(1)} %get-tuple-element.434, pred[2176]{0:T(1024)(128)(4,1)S(1)} %pad_add_fusion.2, f32[128,16]{0,1:T(8,128)S(1)} %bitcast.86), kind=kOutput, calls=%fused_computation.15.clone.1 | convolution fusion | flops 588513280 | bytes 22562944 | tf_op jit(solution)/shard_map/while/body/eval_jaxpr/hqk,khd->qhd/dot_general | solution.py:53
  836.3 8.0 constant_dynamic-slice_fusion.7
  845.6 11.7 %pad_maximum_fusion.5 = (bf16[2176,1024]{1,0:T(8,128)(2,1)}, bf16[2176,1024]{1,0:T(8,128)(2,1)}) fusion(bf16[256,2048]{1,0:T(8,128)(2,1)S(1)} %bitcast.82, bf16[1920,2048]{1,0:T(8,128)(2,1)} %bitcast.76), kind=kLoop, calls=%fused_computation.12.clone.1 | loop fusion | flops 17825792 | bytes 17825792 | tf_op jit(solution)/shard_map/while/body/eval_jaxpr/concatenate | solution.py:113
  857.2 6.5 copy.31
  865.2 10.9 %fusion.47 = (f32[16,128]{1,0:T(8,128)S(1)}, f32[16,128,2176]{2,1,0:T(8,128)}) fusion(pred[2176]{0:T(1024)(128)(4,1)S(1)} %pad_add_fusion.2, bf16[128,16,64]{0,2,1:T(8,128)(2,1)S(1)} %bitcast.83, bf16[2176,16,64]{0,2,1:T(8,128)(2,1)} %bitcast.75), kind=kOutput, calls=%fused_computation.4.clone.1 | convolution fusion | flops 583792640 | bytes 22554752 | tf_op jit(solution)/shard_map/while/body/eval_jaxpr/qhd,khd->hqk/dot_general | solution.py:45
  876.1 9.7 fusion.48
  885.9 6.5 copy.29
  892.4 11.6 %fusion.49 = bf16[128,16,64]{0,2,1:T(8,128)(2,1)S(1)} fusion(bf16[2176,16,64]{0,2,1:T(8,128)(2,1)} %bitcast.81, f32[16,128,2176]{2,1,0:T(8,128)} %get-tuple-element.433, f32[16,128]{1,0:T(8,128)S(1)} %get-tuple-element.434, pred[2176]{0:T(1024)(128)(4,1)S(1)} %pad_add_fusion.2, f32[128,16]{0,1:T(8,128)S(1)} %bitcast.86), kind=kOutput, calls=%fused_computation.15.clone.1 | convolution fusion | flops 588513280 | bytes 22562944 | tf_op jit(solution)/shard_map/while/body/eval_jaxpr/hqk,khd->qhd/dot_general | solution.py:53
  908.1 8.0 constant_dynamic-slice_fusion.7
  917.4 11.7 %pad_maximum_fusion.5 = (bf16[2176,1024]{1,0:T(8,128)(2,1)}, bf16[2176,1024]{1,0:T(8,128)(2,1)}) fusion(bf16[256,2048]{1,0:T(8,128)(2,1)S(1)} %bitcast.82, bf16[1920,2048]{1,0:T(8,128)(2,1)} %bitcast.76), kind=kLoop, calls=%fused_computation.12.clone.1 | loop fusion | flops 17825792 | bytes 17825792 | tf_op jit(solution)/shard_map/while/body/eval_jaxpr/concatenate | solution.py:113
  929.1 6.5 copy.31
  937.0 10.9 %fusion.47 = (f32[16,128]{1,0:T(8,128)S(1)}, f32[16,128,2176]{2,1,0:T(8,128)}) fusion(pred[2176]{0:T(1024)(128)(4,1)S(1)} %pad_add_fusion.2, bf16[128,16,64]{0,2,1:T(8,128)(2,1)S(1)} %bitcast.83, bf16[2176,16,64]{0,2,1:T(8,128)(2,1)} %bitcast.75), kind=kOutput, calls=%fused_computation.4.clone.1 | convolution fusion | flops 583792640 | bytes 22554752 | tf_op jit(solution)/shard_map/while/body/eval_jaxpr/qhd,khd->hqk/dot_general | solution.py:45
  948.0 9.7 fusion.48
  957.7 6.5 copy.29
  964.2 11.6 %fusion.49 = bf16[128,16,64]{0,2,1:T(8,128)(2,1)S(1)} fusion(bf16[2176,16,64]{0,2,1:T(8,128)(2,1)} %bitcast.81, f32[16,128,2176]{2,1,0:T(8,128)} %get-tuple-element.433, f32[16,128]{1,0:T(8,128)S(1)} %get-tuple-element.434, pred[2176]{0:T(1024)(128)(4,1)S(1)} %pad_add_fusion.2, f32[128,16]{0,1:T(8,128)S(1)} %bitcast.86), kind=kOutput, calls=%fused_computation.15.clone.1 | convolution fusion | flops 588513280 | bytes 22562944 | tf_op jit(solution)/shard_map/while/body/eval_jaxpr/hqk,khd->qhd/dot_general | solution.py:53
  976.7 6.7 fusion.23
  (161 shorter events, 79.2 us)
Async XLA Ops:
  6.5 5.1 copy-start
  6.5 4.4 copy-start.4
  6.5 4.4 copy-start.6
  11.7 2.4 copy-start.5
  11.7 2.4 copy-start.7
  25.4 3.4 copy-start.2
  27.2 1.6 collective-permute-start
  28.1 0.7 collective-permute-start.1
  33.6 140.0 %collective-permute-start.2 = (bf16[2,6,128,2048]{3,2,1,0:T(8,128)(2,1)}, bf16[2,6,128,2048]{3,2,1,0:T(8,128)(2,1)}, u32[]{:S(2)}, u32[]{:S(2)}) collective-permute-start(bf16[2,6,128,2048]{3,2,1,0:T(8,128)(2,1)} %pad_maximum_fusion.2), channel_id=1, source_target_pairs={{0,1},{1,2},{2,3},{3,4},{4,5},{5,6},{6,7},{7,8},{8,9},{9,10},{10,1... | collective-permute-start | bytes 18874376 | tf_op jit(solution)/shard_map/ppermute | solution.py:19
  35.5 138.1 %collective-permute-start.3 = (bf16[2,6,128,2048]{3,2,1,0:T(8,128)(2,1)}, bf16[2,6,128,2048]{3,2,1,0:T(8,128)(2,1)}, u32[]{:S(2)}, u32[]{:S(2)}) collective-permute-start(bf16[2,6,128,2048]{3,2,1,0:T(8,128)(2,1)} %pad_maximum_fusion.2), channel_id=1, source_target_pairs={{1,0},{2,1},{3,2},{4,3},{5,4},{6,5},{7,6},{8,7},{9,8},{10,9},{11,1... | collective-permute-start | bytes 18874376 | tf_op jit(solution)/shard_map/ppermute | solution.py:21
  39.2 134.4 %copy-start.3 = (bf16[1024,2048]{1,0:T(8,128)(2,1)S(1)}, bf16[1024,2048]{1,0:T(8,128)(2,1)}, u32[]{:S(2)}) copy-start(bf16[1024,2048]{1,0:T(8,128)(2,1)} %copy.20) | copy-start | bytes 12582916
  45.2 141.2 %copy-start.8 = (s32[2]{0:T(128)S(1)}, s32[2]{0:T(128)}, u32[]{:S(2)}) copy-start(s32[2]{0:T(128)} %param.17) | copy-start | bytes 28
  186.4 105.3 %all-reduce.2.cloned.1.call-start = ((), (), s32[]{:S(2)}) async-start(), calls=%async_computation | async-start | bytes 4194304 | tf_op jit(solution)/shard_map/while/body/eval_jaxpr/psum | solution.py:30
  295.0 104.1 %all-reduce.2.cloned.1.call-start = ((), (), s32[]{:S(2)}) async-start(), calls=%async_computation | async-start | bytes 4194304 | tf_op jit(solution)/shard_map/while/body/eval_jaxpr/psum | solution.py:30
  976.7 6.7 copy-start.1
Sparse Core Ops, SparseCore 0:
  193.5 98.2 all-reduce.1
  302.0 97.0 all-reduce.1
where the time goes:
time: 996 us; the launch traced here: 990 us
  waiting for transfers between devices  324 us (33%)
  local copies, waits for them, and re-layouts  217 us (22%)
  other arithmetic  203 us (20%)
  matrix products  198 us (20%)
  loops' own time  28 us (3%)
  between operations  13.6 us (1%)
    psum x2, waiting for transfers between devices, from_root(): return lax.psum(jnp.where(mine, array, jnp.zeros_like(array)), axis)  196 us
    ppermute x2, waiting for transfers between devices, padded(): lax.ppermute(tail, axis, [(i, (i + 1) % count) for i in range(ends)])  128 us
    concatenate x8, other arithmetic, one_block(): jnp.concatenate([window.reshape(-1, 2 * width_model), keyframe_band.resha...  93.2 us
    dot_general x8, matrix products, attend(): jnp.einsum('hqk,khd->qhd', probs, value_heads, preferred_element_type=jnp...  93 us
    dot_general x8, matrix products, attend(): jnp.einsum('qhd,khd->hqk', query_heads, key_heads, preferred_element_type...  87.3 us
    reduce_sum x8, other arithmetic, attend(): denominator = jnp.sum(weights, axis=-1)  77.7 us
    dynamic_slice x8, local copies, waits for them, and re-layouts, one_block(): lax.dynamic_slice(extended, (frame_local, band_local, 0, 0), (frame_span,...  63.6 us
    slice x8, local copies, waits for them, and re-layouts, attend(): value_heads = key_values[:, width_model:].reshape(-1, head_count, HEAD_DIM)  52.4 us
  transfers between devices with their start and end apart: 6, of which 3 were waited for; matrix products, arithmetic and copies ran while one was open for 1% of the time, Pallas kernels for 0%

commit v1 on v0

--- a/solution.py
+++ b/solution.py
@@ -1,6 +1,11 @@
+import functools
+import math
+
 import jax
 import jax.numpy as jnp
 from jax import lax
+from jax.experimental import pallas as pl
+from jax.experimental.pallas import tpu as pltpu
 from jax.sharding import PartitionSpec as P
 
 HEAD_DIM = 64
@@ -131,9 +136,192 @@
     return updated.astype(jnp.bfloat16).reshape(frame_count, band_count, band_tokens, width_model)
 
 
+LANES = 128
+NEG = -1e30
+
+
+def fused_kernel(
+    frames, bands, band_tokens, keys,
+    valid_ref, left_ref, own_ref, right_ref, key_ref, gain_ref,
+    wq_ref, wk_ref, wv_ref, wo_ref, out_ref,
+    normed, kbuf, vbuf, qbuf, context,
+):
+    step = pl.program_id(0)
+    group = wq_ref.shape[1]
+    frame_rows = bands * band_tokens
+    reach_rows = FRAME_REACH * frame_rows
+    own_rows = frames * frame_rows
+    ext_rows = normed.shape[0]
+    sources = (
+        (left_ref, 0, reach_rows),
+        (own_ref, reach_rows, own_rows),
+        (right_ref, reach_rows + own_rows, reach_rows),
+        (key_ref, 2 * reach_rows + own_rows, keys * frame_rows),
+    )
+
+    @pl.when(step == 0)
+    def _():
+        for source, base, count in sources:
+
+            @pl.loop(0, count // LANES)
+            def _(i):
+                rows = source[pl.ds(pl.multiple_of(i * LANES, LANES), LANES), :].astype(jnp.float32)
+                centred = rows - jnp.mean(rows, axis=-1, keepdims=True)
+                variance = jnp.mean(centred * centred, axis=-1, keepdims=True)
+                normed[pl.ds(pl.multiple_of(base + i * LANES, LANES), LANES), :] = (
+                    centred * lax.rsqrt(variance + 1e-05) * gain_ref[...]
+                ).astype(jnp.bfloat16)
+
+    chunk = 512
+
+    @pl.loop(0, ext_rows // chunk)
+    def _(i):
+        at = pl.ds(pl.multiple_of(i * chunk, chunk), chunk)
+        rows = normed[at, :]
+        kbuf[at, :] = jnp.dot(rows, wk_ref[...], preferred_element_type=jnp.float32).astype(jnp.bfloat16)
+        vbuf[at, :] = jnp.dot(rows, wv_ref[...], preferred_element_type=jnp.float32).astype(jnp.bfloat16)
+
+    @pl.loop(0, own_rows // chunk)
+    def _(i):
+        rows = normed[pl.ds(pl.multiple_of(reach_rows + i * chunk, chunk), chunk), :]
+        q = jnp.dot(rows, wq_ref[...], preferred_element_type=jnp.float32)
+        qbuf[pl.ds(pl.multiple_of(i * chunk, chunk), chunk), :] = (
+            q * (HEAD_DIM ** (-0.5) * math.log2(math.e))
+        ).astype(jnp.bfloat16)
+
+    span = 2 * FRAME_REACH + 1
+    low = lax.broadcasted_iota(jnp.int32, (band_tokens, LANES), 1) < HEAD_DIM
+
+    @pl.loop(0, frames * (group // LANES))
+    def _(number):
+        frame = number // (group // LANES)
+        pair = number % (group // LANES)
+        lanes = pl.ds(pl.multiple_of(pair * LANES, LANES), LANES)
+        for band in range(bands):
+            first = max(band - BAND_REACH, 0)
+            count = min(band + BAND_REACH, bands - 1) + 1 - first
+            at_q = pl.ds(pl.multiple_of(frame * frame_rows + band * band_tokens, band_tokens), band_tokens)
+            q = qbuf[at_q, lanes]
+            zero = jnp.zeros_like(q)
+            q2 = jnp.concatenate([jnp.where(low, q, zero), jnp.where(low, zero, q)], axis=0)
+            places = [
+                pl.ds(
+                    pl.multiple_of((frame + j) * frame_rows + first * band_tokens, band_tokens),
+                    count * band_tokens,
+                )
+                for j in range(span)
+            ] + [
+                pl.ds(2 * reach_rows + own_rows + k * frame_rows + band * band_tokens, band_tokens)
+                for k in range(keys)
+            ]
+            scores = []
+            for j, place in enumerate(places):
+                s = lax.dot_general(
+                    q2, kbuf[place, lanes], (((1,), (1,)), ((), ())),
+                    preferred_element_type=jnp.float32,
+                )
+                if j != FRAME_REACH:
+                    s = jnp.where(valid_ref[frame, j] > 0, s, NEG)
+                scores.append(s)
+            largest = functools.reduce(
+                jnp.maximum, [jnp.max(s, axis=-1, keepdims=True) for s in scores]
+            )
+            total = jnp.zeros((2 * band_tokens, LANES), jnp.float32)
+            denominator = jnp.zeros((2 * band_tokens, 1), jnp.float32)
+            for s, place in zip(scores, places):
+                weights = jnp.exp2(s - largest)
+                denominator += jnp.sum(weights, axis=-1, keepdims=True)
+                total += jnp.dot(
+                    weights.astype(jnp.bfloat16), vbuf[place, lanes],
+                    preferred_element_type=jnp.float32,
+                )
+            total = total / denominator
+            block = jnp.where(low, total[:band_tokens], total[band_tokens:])
+            context[at_q, pl.ds(pl.multiple_of(step * group + pair * LANES, LANES), LANES)] = block.astype(
+                jnp.bfloat16
+            )
+
+    @pl.when(step == pl.num_programs(0) - 1)
+    def _():
+        @pl.loop(0, own_rows // 256)
+        def _(i):
+            at = pl.ds(pl.multiple_of(i * 256, 256), 256)
+            out_ref[at, :] = (
+                own_ref[at, :].astype(jnp.float32)
+                + jnp.dot(context[at, :], wo_ref[...], preferred_element_type=jnp.float32)
+            ).astype(jnp.bfloat16)
+
+
+def fused(tokens, norm_gain, query_weight, key_weight, value_weight, out_weight, key_frames):
+    frame_count, band_count, band_tokens, width_model = tokens.shape
+    frame_rows = band_count * band_tokens
+    keyframe_count = key_frames.shape[0]
+    size = lax.axis_size("tm")
+    me = lax.axis_index("tm")
+    frames_total = size * frame_count
+    left = lax.ppermute(
+        tokens[frame_count - FRAME_REACH:], "tm", [(i, i + 1) for i in range(size - 1)]
+    )
+    right = lax.ppermute(tokens[:FRAME_REACH], "tm", [(i + 1, i) for i in range(size - 1)])
+    first_frame = me * frame_count
+    parts = []
+    for number in range(keyframe_count):
+        target = key_frames[number]
+        local = target - first_frame
+        mine = (local >= 0) & (local < frame_count)
+        part = lax.dynamic_index_in_dim(tokens, jnp.clip(local, 0, frame_count - 1), 0, keepdims=True)
+        parts.append(jnp.where(mine, part, jnp.zeros_like(part)))
+    key_tokens = lax.psum(jnp.concatenate(parts, axis=0), "tm")
+    frame_now = first_frame + jnp.arange(frame_count, dtype=jnp.int32)
+    window = frame_now[:, None] - FRAME_REACH + jnp.arange(2 * FRAME_REACH + 1, dtype=jnp.int32)[None]
+    valid = jnp.concatenate(
+        [
+            (window >= 0) & (window < frames_total),
+            jnp.abs(frame_now[:, None] - key_frames[None]) > FRAME_REACH,
+        ],
+        axis=1,
+    )
+    group = 256
+    ext_rows = (2 * FRAME_REACH + frame_count + keyframe_count) * frame_rows
+    own_rows = frame_count * frame_rows
+    whole = lambda shape: pl.BlockSpec(shape, lambda i: (0, 0), pipeline_mode=pl.Buffered(1))
+    columns = pl.BlockSpec((width_model, group), lambda i: (0, i))
+    out = pl.pallas_call(
+        functools.partial(fused_kernel, frame_count, band_count, band_tokens, keyframe_count),
+        grid=(width_model // group,),
+        out_shape=jax.ShapeDtypeStruct((own_rows, width_model), jnp.bfloat16),
+        in_specs=[
+            pl.BlockSpec(memory_space=pltpu.SMEM),
+            whole((FRAME_REACH * frame_rows, width_model)),
+            whole((own_rows, width_model)),
+            whole((FRAME_REACH * frame_rows, width_model)),
+            whole((keyframe_count * frame_rows, width_model)),
+            whole((1, width_model)),
+            columns, columns, columns,
+            whole((width_model, width_model)),
+        ],
+        out_specs=whole((own_rows, width_model)),
+        scratch_shapes=[
+            pltpu.VMEM((ext_rows, width_model), jnp.bfloat16),
+            pltpu.VMEM((ext_rows, group), jnp.bfloat16),
+            pltpu.VMEM((ext_rows, group), jnp.bfloat16),
+            pltpu.VMEM((own_rows, group), jnp.bfloat16),
+            pltpu.VMEM((own_rows, width_model), jnp.bfloat16),
+        ],
+        compiler_params=pltpu.CompilerParams(vmem_limit_bytes=56 * 2 ** 20),
+    )(
+        valid.astype(jnp.int32),
+        left.reshape(-1, width_model), tokens.reshape(-1, width_model), right.reshape(-1, width_model),
+        key_tokens.reshape(-1, width_model), norm_gain.reshape(1, -1),
+        query_weight, key_weight, value_weight, out_weight,
+    )
+    return out.reshape(tokens.shape)
+
+
 def solution(mesh):
+    body = fused if mesh.shape["band"] == 1 else per_device
     in_specs = (P(("slab", "tm"), "band", None, None), P(), P(), P(), P(), P(), P("slab"))
     out_specs = P(("slab", "tm"), "band", None, None)
     return jax.shard_map(
-        per_device, mesh=mesh, in_specs=in_specs, out_specs=out_specs, check_vma=False
-    )
+        body, mesh=mesh, in_specs=in_specs, out_specs=out_specs, check_vma=False
+    )

time: 996 us -> 229 us (0.23)
  waiting for transfers between devices: 324 us -> 104 us
  local copies, waits for them, and re-layouts: 217 us -> 3.25 us
  other arithmetic: 203 us -> 3.94 us
  matrix products: 198 us -> 0 us
  Pallas kernels: 0 us -> 95.7 us
  loops' own time: 28 us -> 0 us
    dot_general x20 -> x0, matrix products: 198 us -> none  [the longest x8 93 us: attend(): jnp.einsum('hqk,khd->qhd', probs, value_heads, preferred_element_type=jnp...]
    ppermute x4 -> x2, waiting for transfers between devices: 128 us -> 0.01 us  [the longest x1 0.01 us: fused(): lax.ppermute(tokens[frame_count - FRAME_REACH:], 'tm', [(i, i + 1) for i...]
    concatenate x19 -> x1, other arithmetic: 113 us -> 1.5 us  [fused(): key_tokens = lax.psum(jnp.concatenate(parts, axis=0), 'tm')]
    slice x17 -> x1, local copies, waits for them, and re-layouts: 106 us -> 1.38 us  [fused(): target = key_frames[number]]
    pallas_call x0 -> x1, Pallas kernels: none -> 95.7 us  [fused(): pl.pallas_call(functools.partial(fused_kernel, frame_count, band_count, b...]
    psum x2 -> x1, waiting for transfers between devices: 196 us -> 104 us  [fused(): key_tokens = lax.psum(jnp.concatenate(parts, axis=0), 'tm')]
    dynamic_slice x42 -> x0, local copies, waits for them, and re-layouts: 89.1 us -> none  [the longest x8 63.6 us: one_block(): lax.dynamic_slice(extended, (frame_local, band_local, 0, 0), (frame_span,...]
    reduce_sum x10 -> x0, other arithmetic: 82.1 us -> none  [the longest x8 77.7 us: attend(): denominator = jnp.sum(weights, axis=-1)]
  transfers between devices with their start and end apart: 6 -> 3, of which waited for: 3 -> 1; matrix products, arithmetic and copies ran while one was open for 1% -> 2% of each run, Pallas kernels for 0% -> 0%
where the time goes in v1:
time: 229 us; the launch traced here: 227 us
  waiting for transfers between devices  104 us (45%)
  Pallas kernels  95.7 us (42%)
  between operations  14.8 us (6%)
  starting transfers between devices  5.56 us (2%)
  other arithmetic  3.94 us (2%)
  local copies, waits for them, and re-layouts  3.25 us (1%)
    psum x1, waiting for transfers between devices, fused(): key_tokens = lax.psum(jnp.concatenate(parts, axis=0), 'tm')  104 us
    pallas_call x1, Pallas kernels, fused(): pl.pallas_call(functools.partial(fused_kernel, frame_count, band_count, b...  95.7 us
  transfers between devices with their start and end apart: 3, of which 1 were waited for; matrix products, arithmetic and copies ran while one was open for 2% of the time, Pallas kernels for 0%

profile of v1, /device:TPU:6, one launch (start us, length us, event | category | flops | bytes accessed | tf_op | source)
XLA Modules:
  0.0 227.4 jit_solution(10824186233828590433)
XLA Ops:
  6.5 0.0 all-reduce.2.cloned.1.call-start
  6.5 1.9 collective-permute-start
  8.5 3.6 %collective-permute-start.1 = (bf16[2,4,128,1024]{3,2,1,0:T(8,128)(2,1)}, bf16[2,4,128,1024]{3,2,1,0:T(8,128)(2,1)}, u32[]{:S(2)}, u32[]{:S(2)}) collective-permute-start(bf16[2,4,128,1024]{3,2,1,0:T(8,128)(2,1)} %param.7), channel_id=1, source_target_pairs={{1,0},{2,1},{3,2},{4,3},{5,4},{6,5},{7,6},{8,7},{9,8},{10,9},{11,1... | collective-permute-start | bytes 6291464 | tf_op jit(solution)/shard_map/ppermute | solution.py:265
  12.1 1.4 fusion
  14.8 1.7 dynamic-slice_select_fusion.1
  16.5 1.5 pad_maximum_fusion
  18.0 0.0 copy-start.1
  18.0 0.0 all-reduce.2.cloned.1.call-update
  18.1 0.1 compare_and_fusion
  18.1 0.5 copy-done.1
  18.7 0.1 abs_compare_fusion
  18.8 0.6 add_convert_fusion.valid_ref
  19.4 104.2 %all-reduce.2.cloned.1.call-done.key_ref = bf16[1024,1024]{1,0:T(8,128)(2,1)} async-done(((bf16[1024,1024]{1,0:T(8,128)(2,1)}), bf16[1024,1024]{1,0:T(8,128)(2,1)}) %all-reduce.2.cloned.1.call-update) | async-done | bytes 2097168 | tf_op jit(solution)/shard_map/psum | solution.py:274
  123.5 0.0 collective-permute-done
  123.5 0.0 copy-start
  123.6 0.0 collective-permute-done.1
  123.6 1.3 copy-done
  124.9 95.7 %shard_map.73 = bf16[1024,1024]{1,0:T(8,128)(2,1)} custom-call(s32[2,7]{1,0:T(2,128)} %add_convert_fusion.valid_ref, bf16[1024,1024]{1,0:T(8,128)(2,1)} %bitcast.10, bf16[1024,1024]{1,0:T(8,128)(2,1)} %bitcast.9, bf16[1024,1024]{1,0:T(8,128)(2,1)} %bitcast.2.right_ref, bf16[1024,1024]{1,0:T(8,128)(2,1)} %all-reduce.2.cloned.1.call-done.key_ref, ...), custom_call_target="tpu_custom_call" | custom-call | tf_op jit(solution)/shard_map/pallas_call | solution.py:289
  (1 shorter events, 0.0 us)
Async XLA Ops:
  6.5 117.0 %all-reduce.2.cloned.1.call-start = ((), (), s32[]{:S(2)}) async-start(), calls=%async_computation | async-start | bytes 4194304 | tf_op jit(solution)/shard_map/psum | solution.py:274
  6.5 117.0 %collective-permute-start = (bf16[2,4,128,1024]{3,2,1,0:T(8,128)(2,1)}, bf16[2,4,128,1024]{3,2,1,0:T(8,128)(2,1)S(1)}, u32[]{:S(2)}, u32[]{:S(2)}) collective-permute-start(bf16[2,4,128,1024]{3,2,1,0:T(8,128)(2,1)} %param.7), channel_id=1, source_target_pairs={{0,1},{1,2},{2,3},{3,4},{4,5},{5,6},{6,7},{7,8},{8,9},{9,10},{10,1... | collective-permute-start | bytes 6291464 | tf_op jit(solution)/shard_map/ppermute | solution.py:262
  8.5 115.1 %collective-permute-start.1 = (bf16[2,4,128,1024]{3,2,1,0:T(8,128)(2,1)}, bf16[2,4,128,1024]{3,2,1,0:T(8,128)(2,1)}, u32[]{:S(2)}, u32[]{:S(2)}) collective-permute-start(bf16[2,4,128,1024]{3,2,1,0:T(8,128)(2,1)} %param.7), channel_id=1, source_target_pairs={{1,0},{2,1},{3,2},{4,3},{5,4},{6,5},{7,6},{8,7},{9,8},{10,9},{11,1... | collective-permute-start | bytes 6291464 | tf_op jit(solution)/shard_map/ppermute | solution.py:265
  18.0 0.7 copy-start.1
  123.5 1.3 copy-start
Sparse Core Ops, SparseCore 0:
  18.2 105.3 all-reduce.1

commit v2 on v1

--- a/solution.py
+++ b/solution.py
@@ -143,18 +143,16 @@
 def fused_kernel(
     frames, bands, band_tokens, keys,
     valid_ref, left_ref, own_ref, right_ref, key_ref, gain_ref,
-    wq_ref, wk_ref, wv_ref, wo_ref, out_ref,
-    normed, kbuf, vbuf, qbuf, context,
+    q_ref, k_ref, v_ref, wk_ref, wv_ref, wo_ref, out_ref,
+    normed, kbuf, vbuf, context,
 ):
     step = pl.program_id(0)
-    group = wq_ref.shape[1]
+    group = wk_ref.shape[1]
     frame_rows = bands * band_tokens
     reach_rows = FRAME_REACH * frame_rows
     own_rows = frames * frame_rows
-    ext_rows = normed.shape[0]
     sources = (
         (left_ref, 0, reach_rows),
-        (own_ref, reach_rows, own_rows),
         (right_ref, reach_rows + own_rows, reach_rows),
         (key_ref, 2 * reach_rows + own_rows, keys * frame_rows),
     )
@@ -165,29 +163,21 @@
 
             @pl.loop(0, count // LANES)
             def _(i):
-                rows = source[pl.ds(pl.multiple_of(i * LANES, LANES), LANES), :].astype(jnp.float32)
-                centred = rows - jnp.mean(rows, axis=-1, keepdims=True)
-                variance = jnp.mean(centred * centred, axis=-1, keepdims=True)
-                normed[pl.ds(pl.multiple_of(base + i * LANES, LANES), LANES), :] = (
-                    centred * lax.rsqrt(variance + 1e-05) * gain_ref[...]
-                ).astype(jnp.bfloat16)
+                rows = source[pl.ds(pl.multiple_of(i * LANES, LANES), LANES), :]
+                normed[pl.ds(pl.multiple_of(base + i * LANES, LANES), LANES), :] = normalise(rows, gain_ref[...])
 
     chunk = 512
-
-    @pl.loop(0, ext_rows // chunk)
-    def _(i):
-        at = pl.ds(pl.multiple_of(i * chunk, chunk), chunk)
-        rows = normed[at, :]
-        kbuf[at, :] = jnp.dot(rows, wk_ref[...], preferred_element_type=jnp.float32).astype(jnp.bfloat16)
-        vbuf[at, :] = jnp.dot(rows, wv_ref[...], preferred_element_type=jnp.float32).astype(jnp.bfloat16)
-
-    @pl.loop(0, own_rows // chunk)
-    def _(i):
-        rows = normed[pl.ds(pl.multiple_of(reach_rows + i * chunk, chunk), chunk), :]
-        q = jnp.dot(rows, wq_ref[...], preferred_element_type=jnp.float32)
-        qbuf[pl.ds(pl.multiple_of(i * chunk, chunk), chunk), :] = (
-            q * (HEAD_DIM ** (-0.5) * math.log2(math.e))
-        ).astype(jnp.bfloat16)
+    for _, base, count in sources:
+
+        @pl.loop(0, count // chunk)
+        def _(i):
+            at = pl.ds(pl.multiple_of(base + i * chunk, chunk), chunk)
+            rows = normed[at, :]
+            kbuf[at, :] = jnp.dot(rows, wk_ref[...], preferred_element_type=jnp.float32).astype(jnp.bfloat16)
+            vbuf[at, :] = jnp.dot(rows, wv_ref[...], preferred_element_type=jnp.float32).astype(jnp.bfloat16)
+
+    kbuf[pl.ds(reach_rows, own_rows), :] = k_ref[...]
+    vbuf[pl.ds(reach_rows, own_rows), :] = v_ref[...]
 
     span = 2 * FRAME_REACH + 1
     low = lax.broadcasted_iota(jnp.int32, (band_tokens, LANES), 1) < HEAD_DIM
@@ -201,7 +191,7 @@
             first = max(band - BAND_REACH, 0)
             count = min(band + BAND_REACH, bands - 1) + 1 - first
             at_q = pl.ds(pl.multiple_of(frame * frame_rows + band * band_tokens, band_tokens), band_tokens)
-            q = qbuf[at_q, lanes]
+            q = q_ref[at_q, lanes]
             zero = jnp.zeros_like(q)
             q2 = jnp.concatenate([jnp.where(low, q, zero), jnp.where(low, zero, q)], axis=0)
             places = [
@@ -252,6 +242,204 @@
             ).astype(jnp.bfloat16)
 
 
+KEY_CHUNKS = 4
+
+
+def normalise(rows, gain):
+    rows = rows.astype(jnp.float32)
+    centred = rows - jnp.mean(rows, axis=-1, keepdims=True)
+    variance = jnp.mean(centred * centred, axis=-1, keepdims=True)
+    return (centred * lax.rsqrt(variance + 1e-05) * gain).astype(jnp.bfloat16)
+
+
+def exchange_kernel(
+    size, frame_rows,
+    tokens_ref, gain_ref, wq_hbm, wk_hbm, wv_hbm,
+    left_ref, right_ref, key_ref, q_ref, k_ref, v_ref,
+    own, wq, wk, wv, halo_send, halo_recv, key_send, key_recv, local_sem, edge_sem, root_sem,
+):
+    me = lax.axis_index("tm")
+    place = lax.rem(me, 4)
+    own_rows = tokens_ref.shape[0]
+    reach_rows = FRAME_REACH * frame_rows
+    across = jnp.where(place < 2, me + 2, me - 2)
+    corner = (place == 0) | (place == 3)
+    partners = (
+        (me > 0, me - 1),
+        (me < size - 1, me + 1),
+        (me >= 0, across),
+        (corner & (me >= 4), me - 4),
+        (corner & (me < size - 4), me + 4),
+    )
+    barrier = pltpu.get_barrier_semaphore()
+    expected = 0
+    for there, device in partners:
+        expected = expected + jnp.where(there, 1, 0)
+
+        @pl.when(there)
+        def _():
+            pl.semaphore_signal(
+                barrier, inc=1, device_id={"tm": device}, device_id_type=pl.DeviceIdType.MESH
+            )
+
+    pl.semaphore_wait(barrier, expected)
+
+    part = frame_rows // KEY_CHUNKS
+
+    def children(k):
+        j = me if k == 0 else size - 1 - me
+        sign = 1 if k == 0 else -1
+        r = lax.rem(j, 4)
+        return j, (
+            ((r == 0) & (j < size - 4), me + 4 * sign),
+            (r == 0, me + 2 * sign),
+            (lax.rem(j, 2) == 0, me + sign),
+        )
+
+    def key_copy(k, c, child, device, source, base):
+        return pltpu.make_async_remote_copy(
+            src_ref=source.at[pl.ds(base + c * part, part), :],
+            dst_ref=key_ref.at[pl.ds(k * frame_rows + c * part, part), :],
+            send_sem=key_send.at[k, c, child],
+            recv_sem=key_recv.at[k, c],
+            device_id={"tm": device},
+            device_id_type=pl.DeviceIdType.MESH,
+        )
+
+    for k in range(2):
+        j, targets = children(k)
+        base = 0 if k == 0 else own_rows - frame_rows
+
+        @pl.when(j == 0)
+        def _():
+            for c in range(KEY_CHUNKS):
+                for child, (there, device) in enumerate(targets):
+                    key_copy(k, c, child, device, tokens_ref, base).start()
+            pltpu.make_async_copy(
+                tokens_ref.at[pl.ds(base, frame_rows), :],
+                key_ref.at[pl.ds(k * frame_rows, frame_rows), :],
+                root_sem.at[k],
+            ).start()
+
+    halos = []
+    for side, (there, device, base, target) in enumerate((
+        (me < size - 1, me + 1, own_rows - reach_rows, left_ref),
+        (me > 0, me - 1, 0, right_ref),
+    )):
+        remote = pltpu.make_async_remote_copy(
+            src_ref=tokens_ref.at[pl.ds(base, reach_rows), :],
+            dst_ref=target,
+            send_sem=halo_send.at[side],
+            recv_sem=halo_recv.at[side],
+            device_id={"tm": device},
+            device_id_type=pl.DeviceIdType.MESH,
+        )
+        edge = pltpu.make_async_copy(
+            tokens_ref.at[pl.ds(base, reach_rows), :], target, edge_sem.at[side]
+        )
+        receives = me > 0 if side == 0 else me < size - 1
+        halos.append((there, receives, remote, edge))
+
+        @pl.when(there)
+        def _():
+            remote.start()
+
+        @pl.when(jnp.logical_not(receives))
+        def _():
+            edge.start()
+
+    loads = [
+        pltpu.make_async_copy(source, target, local_sem.at[i])
+        for i, (source, target) in enumerate(
+            ((tokens_ref, own), (wq_hbm, wq), (wk_hbm, wk), (wv_hbm, wv))
+        )
+    ]
+    for load in loads:
+        load.start()
+    for load in loads:
+        load.wait()
+
+    step_rows = own_rows // KEY_CHUNKS
+    for c in range(KEY_CHUNKS):
+        for k in range(2):
+            j, targets = children(k)
+
+            @pl.when(j > 0)
+            def _():
+                key_copy(k, c, 0, across, key_ref, k * frame_rows).wait_recv()
+                for child, (there, device) in enumerate(targets):
+
+                    @pl.when(there)
+                    def _():
+                        key_copy(k, c, child, device, key_ref, k * frame_rows).start()
+
+        at = pl.ds(c * step_rows, step_rows)
+        rows = normalise(own[at, :], gain_ref[...])
+        q = jnp.dot(rows, wq[...], preferred_element_type=jnp.float32)
+        q_ref[at, :] = (q * (HEAD_DIM ** (-0.5) * math.log2(math.e))).astype(jnp.bfloat16)
+        k_ref[at, :] = jnp.dot(rows, wk[...], preferred_element_type=jnp.float32).astype(jnp.bfloat16)
+        v_ref[at, :] = jnp.dot(rows, wv[...], preferred_element_type=jnp.float32).astype(jnp.bfloat16)
+
+    for there, receives, remote, edge in halos:
+
+        @pl.when(receives)
+        def _():
+            remote.wait_recv()
+
+        @pl.when(jnp.logical_not(receives))
+        def _():
+            edge.wait()
+
+        @pl.when(there)
+        def _():
+            remote.wait_send()
+
+    for k in range(2):
+        j, targets = children(k)
+
+        @pl.when(j == 0)
+        def _():
+            pltpu.make_async_copy(
+                tokens_ref.at[pl.ds(0, frame_rows), :],
+                key_ref.at[pl.ds(k * frame_rows, frame_rows), :],
+                root_sem.at[k],
+            ).wait()
+
+        for c in range(KEY_CHUNKS):
+            for child, (there, device) in enumerate(targets):
+
+                @pl.when(there)
+                def _():
+                    key_copy(k, c, child, device, key_ref, k * frame_rows).wait_send()
+
+
+def exchange(token_rows, gain, query_weight, key_weight, value_weight, size, frame_rows):
+    own_rows, width = token_rows.shape
+    shape = lambda rows: jax.ShapeDtypeStruct((rows, width), jnp.bfloat16)
+    hbm = pl.BlockSpec(memory_space=pl.ANY)
+    vmem = pl.BlockSpec(memory_space=pltpu.VMEM)
+    reach_rows = FRAME_REACH * frame_rows
+    dma = pltpu.SemaphoreType.DMA
+    square = pltpu.VMEM((width, width), jnp.bfloat16)
+    return pl.pallas_call(
+        functools.partial(exchange_kernel, size, frame_rows),
+        out_shape=(
+            shape(reach_rows), shape(reach_rows), shape(2 * frame_rows),
+            shape(own_rows), shape(own_rows), shape(own_rows),
+        ),
+        in_specs=[hbm, vmem, hbm, hbm, hbm],
+        out_specs=(hbm, hbm, hbm, vmem, vmem, vmem),
+        scratch_shapes=[
+            pltpu.VMEM((own_rows, width), jnp.bfloat16), square, square, square,
+            dma((2,)), dma((2,)), dma((2, KEY_CHUNKS, 3)), dma((2, KEY_CHUNKS)),
+            dma((4,)), dma((2,)), dma((2,)),
+        ],
+        compiler_params=pltpu.CompilerParams(
+            collective_id=0, has_side_effects=True, vmem_limit_bytes=40 * 2 ** 20
+        ),
+    )(token_rows, gain, query_weight, key_weight, value_weight)
+
+
 def fused(tokens, norm_gain, query_weight, key_weight, value_weight, out_weight, key_frames):
     frame_count, band_count, band_tokens, width_model = tokens.shape
     frame_rows = band_count * band_tokens
@@ -259,19 +447,12 @@
     size = lax.axis_size("tm")
     me = lax.axis_index("tm")
     frames_total = size * frame_count
-    left = lax.ppermute(
-        tokens[frame_count - FRAME_REACH:], "tm", [(i, i + 1) for i in range(size - 1)]
-    )
-    right = lax.ppermute(tokens[:FRAME_REACH], "tm", [(i + 1, i) for i in range(size - 1)])
+    token_rows = tokens.reshape(-1, width_model)
+    gain = norm_gain.reshape(1, -1)
+    left, right, key_tokens, queries, key_rows, values = exchange(
+        token_rows, gain, query_weight, key_weight, value_weight, size, frame_rows
+    )
     first_frame = me * frame_count
-    parts = []
-    for number in range(keyframe_count):
-        target = key_frames[number]
-        local = target - first_frame
-        mine = (local >= 0) & (local < frame_count)
-        part = lax.dynamic_index_in_dim(tokens, jnp.clip(local, 0, frame_count - 1), 0, keepdims=True)
-        parts.append(jnp.where(mine, part, jnp.zeros_like(part)))
-    key_tokens = lax.psum(jnp.concatenate(parts, axis=0), "tm")
     frame_now = first_frame + jnp.arange(frame_count, dtype=jnp.int32)
     window = frame_now[:, None] - FRAME_REACH + jnp.arange(2 * FRAME_REACH + 1, dtype=jnp.int32)[None]
     valid = jnp.concatenate(
@@ -286,6 +467,7 @@
     own_rows = frame_count * frame_rows
     whole = lambda shape: pl.BlockSpec(shape, lambda i: (0, 0), pipeline_mode=pl.Buffered(1))
     columns = pl.BlockSpec((width_model, group), lambda i: (0, i))
+    own_columns = pl.BlockSpec((own_rows, group), lambda i: (0, i))
     out = pl.pallas_call(
         functools.partial(fused_kernel, frame_count, band_count, band_tokens, keyframe_count),
         grid=(width_model // group,),
@@ -297,7 +479,8 @@
             whole((FRAME_REACH * frame_rows, width_model)),
             whole((keyframe_count * frame_rows, width_model)),
             whole((1, width_model)),
-            columns, columns, columns,
+            own_columns, own_columns, own_columns,
+            columns, columns,
             whole((width_model, width_model)),
         ],
         out_specs=whole((own_rows, width_model)),
@@ -305,21 +488,26 @@
             pltpu.VMEM((ext_rows, width_model), jnp.bfloat16),
             pltpu.VMEM((ext_rows, group), jnp.bfloat16),
             pltpu.VMEM((ext_rows, group), jnp.bfloat16),
-            pltpu.VMEM((own_rows, group), jnp.bfloat16),
             pltpu.VMEM((own_rows, width_model), jnp.bfloat16),
         ],
         compiler_params=pltpu.CompilerParams(vmem_limit_bytes=56 * 2 ** 20),
     )(
         valid.astype(jnp.int32),
-        left.reshape(-1, width_model), tokens.reshape(-1, width_model), right.reshape(-1, width_model),
-        key_tokens.reshape(-1, width_model), norm_gain.reshape(1, -1),
-        query_weight, key_weight, value_weight, out_weight,
+        left, token_rows, right, key_tokens, gain,
+        queries, key_rows, values, key_weight, value_weight, out_weight,
     )
     return out.reshape(tokens.shape)
 
 
 def solution(mesh):
-    body = fused if mesh.shape["band"] == 1 else per_device
+    simple = mesh.shape["band"] == 1 and mesh.shape["tm"] % 4 == 0
+
+    def body(*args):
+        frames, keys = args[0].shape[0], args[6].shape[0]
+        if simple and frames >= FRAME_REACH and keys == 2:
+            return fused(*args)
+        return per_device(*args)
+
     in_specs = (P(("slab", "tm"), "band", None, None), P(), P(), P(), P(), P(), P("slab"))
     out_specs = P(("slab", "tm"), "band", None, None)
     return jax.shard_map(

time: 229 us -> 227 us (level)
  the two profiles are of different devices: /device:TPU:6 before, /device:TPU:0 now
where the time goes in v2:
time: 227 us; the launch traced here: 226 us
  Pallas kernels  216 us (95%)
  local copies, waits for them, and re-layouts  8.69 us (4%)
    pallas_call x1, Pallas kernels, exchange(): pl.pallas_call(functools.partial(exchange_kernel, size, frame_rows), out_...  131 us
    pallas_call x1, Pallas kernels, fused(): pl.pallas_call(functools.partial(fused_kernel, frame_count, band_count, b...  85.5 us
    unnamed x14, local copies, waits for them, and re-layouts  8.69 us

profile of v2, /device:TPU:0, one launch (start us, length us, event | category | flops | bytes accessed | tf_op | source)
XLA Modules:
  0.0 226.4 jit_solution(9571117111381427002)
XLA Ops:
  0.0 0.7 abs_compare_fusion
  0.7 0.1 compare_and_fusion
  0.8 0.6 add_convert_fusion.valid_ref
  1.4 0.0 copy-start.6
  1.4 0.7 copy-done.6
  2.1 130.8 %shard_map.73 = (bf16[1024,1024]{1,0:T(8,128)(2,1)S(1)}, bf16[1024,1024]{1,0:T(8,128)(2,1)S(1)}, bf16[1024,1024]{1,0:T(8,128)(2,1)S(1)}, bf16[1024,1024]{1,0:T(8...) custom-call(bf16[1024,1024]{1,0:T(8,128)(2,1)} %bitcast.5, f32[1,1024]{1,0:T(1,128)S(1)} %bitcast.4, ...), custom_call_target="tpu_custom_call" | custom-call | tf_op jit(solution)/shard_map/pallas_call | solution.py:424
  132.9 0.0 copy-start
  132.9 1.3 copy-done
  134.2 0.0 copy-start.1
  134.2 1.3 copy-done.1
  135.5 0.0 copy-start.2
  135.5 1.3 copy-done.2
  136.9 0.0 copy-start.3
  136.9 1.4 copy-done.3
  138.2 0.0 copy-start.4
  138.2 1.4 copy-done.4
  139.6 0.0 copy-start.5
  139.6 1.3 copy-done.5
  140.9 85.5 %shard_map.74 = bf16[1024,1024]{1,0:T(8,128)(2,1)} custom-call(s32[2,7]{1,0:T(2,128)} %add_convert_fusion.valid_ref, bf16[1024,1024]{1,0:T(8,128)(2,1)} %copy-done, bf16[1024,1024]{1,0:T(8,128)(2,1)} %bitcast.6, bf16[1024,1024]{1,0:T(8,128)(2,1)} %copy-done.1, bf16[1024,1024]{1,0:T(8,128)(2,1)} %copy-done.2, f32[1,1024]{1,0:T(1,128)} %bitcast.3, ...), custom_call_target="tpu_custom_call" | custom-call | tf_op jit(solution)/shard_map/pallas_call | solution.py:471
  (1 shorter events, 0.0 us)
Async XLA Ops:
  1.4 0.7 copy-start.6
  132.9 1.3 copy-start
  134.2 1.3 copy-start.1
  135.5 1.3 copy-start.2
  136.9 1.4 copy-start.3
  138.2 1.4 copy-start.4
  139.6 1.3 copy-start.5

commit v3 on v2

--- a/solution.py
+++ b/solution.py
@@ -359,19 +359,40 @@
     for load in loads:
         load.wait()
 
+    def forward(k, c):
+        j, targets = children(k)
+
+        @pl.when(j > 0)
+        def _():
+            key_copy(k, c, 0, across, key_ref, k * frame_rows).wait_recv()
+            for child, (there, device) in enumerate(targets):
+
+                @pl.when(there)
+                def _():
+                    key_copy(k, c, child, device, key_ref, k * frame_rows).start()
+
+    near_first = me < size // 2
+
+    @pl.when(near_first)
+    def _():
+        for c in range(KEY_CHUNKS):
+            forward(0, c)
+
+    @pl.when(jnp.logical_not(near_first))
+    def _():
+        for c in range(KEY_CHUNKS):
+            forward(1, c)
+
     step_rows = own_rows // KEY_CHUNKS
     for c in range(KEY_CHUNKS):
-        for k in range(2):
-            j, targets = children(k)
-
-            @pl.when(j > 0)
-            def _():
-                key_copy(k, c, 0, across, key_ref, k * frame_rows).wait_recv()
-                for child, (there, device) in enumerate(targets):
-
-                    @pl.when(there)
-                    def _():
-                        key_copy(k, c, child, device, key_ref, k * frame_rows).start()
+
+        @pl.when(near_first)
+        def _():
+            forward(1, c)
+
+        @pl.when(jnp.logical_not(near_first))
+        def _():
+            forward(0, c)
 
         at = pl.ds(c * step_rows, step_rows)
         rows = normalise(own[at, :], gain_ref[...])

time: 227 us -> 171 us (0.75)
  Pallas kernels: 216 us -> 161 us
    pallas_call x1, Pallas kernels: 131 us -> 75.2 us  [exchange(): pl.pallas_call(functools.partial(exchange_kernel, size, frame_rows), out_...]
where the time goes in v3:
time: 171 us
  Pallas kernels  161 us (94%)
  local copies, waits for them, and re-layouts  8.69 us (5%)
    pallas_call x1, Pallas kernels, fused(): pl.pallas_call(functools.partial(fused_kernel, frame_count, band_count, b...  85.5 us
    pallas_call x1, Pallas kernels, exchange(): pl.pallas_call(functools.partial(exchange_kernel, size, frame_rows), out_...  75.2 us
    unnamed x14, local copies, waits for them, and re-layouts  8.69 us

profile of v3, /device:TPU:0, one launch (start us, length us, event | category | flops | bytes accessed | tf_op | source)
XLA Modules:
  0.0 170.8 jit_solution(15506043980171602324)
XLA Ops:
  0.0 0.7 abs_compare_fusion
  0.7 0.1 compare_and_fusion
  0.8 0.6 add_convert_fusion.valid_ref
  1.4 0.0 copy-start.6
  1.4 0.7 copy-done.6
  2.1 75.2 %shard_map.73 = (bf16[1024,1024]{1,0:T(8,128)(2,1)S(1)}, bf16[1024,1024]{1,0:T(8,128)(2,1)S(1)}, bf16[1024,1024]{1,0:T(8,128)(2,1)S(1)}, bf16[1024,1024]{1,0:T(8...) custom-call(bf16[1024,1024]{1,0:T(8,128)(2,1)} %bitcast.5, f32[1,1024]{1,0:T(1,128)S(1)} %bitcast.4, ...), custom_call_target="tpu_custom_call" | custom-call | tf_op jit(solution)/shard_map/pallas_call | solution.py:445
  77.3 0.0 copy-start
  77.3 1.3 copy-done
  78.7 0.0 copy-start.1
  78.7 1.3 copy-done.1
  80.0 0.0 copy-start.2
  80.0 1.3 copy-done.2
  81.3 0.0 copy-start.3
  81.3 1.4 copy-done.3
  82.6 0.0 copy-start.4
  82.6 1.4 copy-done.4
  84.0 0.0 copy-start.5
  84.0 1.3 copy-done.5
  85.3 85.5 %shard_map.74 = bf16[1024,1024]{1,0:T(8,128)(2,1)} custom-call(s32[2,7]{1,0:T(2,128)} %add_convert_fusion.valid_ref, bf16[1024,1024]{1,0:T(8,128)(2,1)} %copy-done, bf16[1024,1024]{1,0:T(8,128)(2,1)} %bitcast.6, bf16[1024,1024]{1,0:T(8,128)(2,1)} %copy-done.1, bf16[1024,1024]{1,0:T(8,128)(2,1)} %copy-done.2, f32[1,1024]{1,0:T(1,128)} %bitcast.3, ...), custom_call_target="tpu_custom_call" | custom-call | tf_op jit(solution)/shard_map/pallas_call | solution.py:492
  (1 shorter events, 0.0 us)
Async XLA Ops:
  1.4 0.7 copy-start.6
  77.3 1.3 copy-start
  78.7 1.3 copy-start.1
  80.0 1.3 copy-start.2
  81.3 1.4 copy-start.3
  82.6 1.4 copy-start.4
  84.0 1.3 copy-start.5

commit v4 on v3

--- a/solution.py
+++ b/solution.py
@@ -213,20 +213,24 @@
                 if j != FRAME_REACH:
                     s = jnp.where(valid_ref[frame, j] > 0, s, NEG)
                 scores.append(s)
-            largest = functools.reduce(
-                jnp.maximum, [jnp.max(s, axis=-1, keepdims=True) for s in scores]
+            split = lambda s: [s[:, i : i + LANES] for i in range(0, s.shape[1], LANES)]
+            largest = jnp.max(
+                functools.reduce(jnp.maximum, sum([split(s) for s in scores], [])),
+                axis=-1, keepdims=True,
             )
             total = jnp.zeros((2 * band_tokens, LANES), jnp.float32)
-            denominator = jnp.zeros((2 * band_tokens, 1), jnp.float32)
+            lane_sums = jnp.zeros((2 * band_tokens, LANES), jnp.float32)
             for s, place in zip(scores, places):
                 weights = jnp.exp2(s - largest)
-                denominator += jnp.sum(weights, axis=-1, keepdims=True)
+                lane_sums += functools.reduce(jnp.add, split(weights))
                 total += jnp.dot(
                     weights.astype(jnp.bfloat16), vbuf[place, lanes],
                     preferred_element_type=jnp.float32,
                 )
-            total = total / denominator
-            block = jnp.where(low, total[:band_tokens], total[band_tokens:])
+            denominator = jnp.sum(lane_sums, axis=-1, keepdims=True)
+            block = jnp.where(low, total[:band_tokens], total[band_tokens:]) / jnp.where(
+                low, denominator[:band_tokens], denominator[band_tokens:]
+            )
             context[at_q, pl.ds(pl.multiple_of(step * group + pair * LANES, LANES), LANES)] = block.astype(
                 jnp.bfloat16
             )
@@ -263,13 +267,12 @@
     own_rows = tokens_ref.shape[0]
     reach_rows = FRAME_REACH * frame_rows
     across = jnp.where(place < 2, me + 2, me - 2)
-    corner = (place == 0) | (place == 3)
     partners = (
         (me > 0, me - 1),
         (me < size - 1, me + 1),
         (me >= 0, across),
-        (corner & (me >= 4), me - 4),
-        (corner & (me < size - 4), me + 4),
+        (me >= 4, me - 4),
+        (me < size - 4, me + 4),
     )
     barrier = pltpu.get_barrier_semaphore()
     expected = 0
@@ -289,10 +292,9 @@
     def children(k):
         j = me if k == 0 else size - 1 - me
         sign = 1 if k == 0 else -1
-        r = lax.rem(j, 4)
         return j, (
-            ((r == 0) & (j < size - 4), me + 4 * sign),
-            (r == 0, me + 2 * sign),
+            ((lax.rem(j, 2) == 0) & (j < size - 4), me + 4 * sign),
+            (j == 0, me + 2 * sign),
             (lax.rem(j, 2) == 0, me + sign),
         )
 

time: 171 us -> 168 us (0.982)
  the two profiles are of different devices: /device:TPU:0 before, /device:TPU:6 now
where the time goes in v4:
time: 168 us
  Pallas kernels  158 us (94%)
  local copies, waits for them, and re-layouts  8.69 us (5%)
    pallas_call x1, Pallas kernels, fused(): pl.pallas_call(functools.partial(fused_kernel, frame_count, band_count, b...  85.7 us
    pallas_call x1, Pallas kernels, exchange(): pl.pallas_call(functools.partial(exchange_kernel, size, frame_rows), out_...  72.1 us
    unnamed x14, local copies, waits for them, and re-layouts  8.69 us

profile of v4, /device:TPU:6, one launch (start us, length us, event | category | flops | bytes accessed | tf_op | source)
XLA Modules:
  0.0 167.9 jit_solution(4699912762986906969)
XLA Ops:
  0.0 0.7 abs_compare_fusion
  0.7 0.1 compare_and_fusion
  0.8 0.6 add_convert_fusion.valid_ref
  1.4 0.0 copy-start.6
  1.4 0.7 copy-done.6
  2.1 72.1 %shard_map.73 = (bf16[1024,1024]{1,0:T(8,128)(2,1)S(1)}, bf16[1024,1024]{1,0:T(8,128)(2,1)S(1)}, bf16[1024,1024]{1,0:T(8,128)(2,1)S(1)}, bf16[1024,1024]{1,0:T(8...) custom-call(bf16[1024,1024]{1,0:T(8,128)(2,1)} %bitcast.5, f32[1,1024]{1,0:T(1,128)S(1)} %bitcast.4, ...), custom_call_target="tpu_custom_call" | custom-call | tf_op jit(solution)/shard_map/pallas_call | solution.py:447
  74.2 0.0 copy-start
  74.2 1.3 copy-done
  75.5 0.0 copy-start.1
  75.5 1.3 copy-done.1
  76.8 0.0 copy-start.2
  76.8 1.3 copy-done.2
  78.2 0.0 copy-start.3
  78.2 1.4 copy-done.3
  79.5 0.0 copy-start.4
  79.5 1.4 copy-done.4
  80.9 0.0 copy-start.5
  80.9 1.3 copy-done.5
  82.2 85.7 %shard_map.74 = bf16[1024,1024]{1,0:T(8,128)(2,1)} custom-call(s32[2,7]{1,0:T(2,128)} %add_convert_fusion.valid_ref, bf16[1024,1024]{1,0:T(8,128)(2,1)} %copy-done, bf16[1024,1024]{1,0:T(8,128)(2,1)} %bitcast.6, bf16[1024,1024]{1,0:T(8,128)(2,1)} %copy-done.1, bf16[1024,1024]{1,0:T(8,128)(2,1)} %copy-done.2, f32[1,1024]{1,0:T(1,128)} %bitcast.3, ...), custom_call_target="tpu_custom_call" | custom-call | tf_op jit(solution)/shard_map/pallas_call | solution.py:494
  (1 shorter events, 0.0 us)
Async XLA Ops:
  1.4 0.7 copy-start.6
  74.2 1.3 copy-start
  75.5 1.3 copy-start.1
  76.8 1.3 copy-start.2
  78.2 1.4 copy-start.3
  79.5 1.4 copy-start.4
  80.9 1.3 copy-start.5

commit v5 on v4

--- a/solution.py
+++ b/solution.py
@@ -246,7 +246,8 @@
             ).astype(jnp.bfloat16)
 
 
-KEY_CHUNKS = 4
+KEY_CHUNKS = 8
+PROJECTIONS = 4
 
 
 def normalise(rows, gain):
@@ -385,7 +386,8 @@
         for c in range(KEY_CHUNKS):
             forward(1, c)
 
-    step_rows = own_rows // KEY_CHUNKS
+    step_rows = own_rows // PROJECTIONS
+    every = KEY_CHUNKS // PROJECTIONS
     for c in range(KEY_CHUNKS):
 
         @pl.when(near_first)
@@ -396,7 +398,9 @@
         def _():
             forward(0, c)
 
-        at = pl.ds(c * step_rows, step_rows)
+        if c % every != every - 1:
+            continue
+        at = pl.ds(c // every * step_rows, step_rows)
         rows = normalise(own[at, :], gain_ref[...])
         q = jnp.dot(rows, wq[...], preferred_element_type=jnp.float32)
         q_ref[at, :] = (q * (HEAD_DIM ** (-0.5) * math.log2(math.e))).astype(jnp.bfloat16)

time: 168 us -> 167 us (level)
  Pallas kernels: 158 us -> 156 us
where the time goes in v5:
time: 167 us; the launch traced here: 166 us
  Pallas kernels  156 us (93%)
  local copies, waits for them, and re-layouts  8.69 us (5%)
    pallas_call x1, Pallas kernels, fused(): pl.pallas_call(functools.partial(fused_kernel, frame_count, band_count, b...  85.7 us
    pallas_call x1, Pallas kernels, exchange(): pl.pallas_call(functools.partial(exchange_kernel, size, frame_rows), out_...  70.6 us
    unnamed x14, local copies, waits for them, and re-layouts  8.69 us

profile of v5, /device:TPU:6, one launch (start us, length us, event | category | flops | bytes accessed | tf_op | source)
XLA Modules:
  0.0 166.4 jit_solution(15701998039578953450)
XLA Ops:
  0.0 0.7 abs_compare_fusion
  0.7 0.1 compare_and_fusion
  0.8 0.6 add_convert_fusion.valid_ref
  1.4 0.0 copy-start.6
  1.4 0.7 copy-done.6
  2.1 70.6 %shard_map.73 = (bf16[1024,1024]{1,0:T(8,128)(2,1)S(1)}, bf16[1024,1024]{1,0:T(8,128)(2,1)S(1)}, bf16[1024,1024]{1,0:T(8,128)(2,1)S(1)}, bf16[1024,1024]{1,0:T(8...) custom-call(bf16[1024,1024]{1,0:T(8,128)(2,1)} %bitcast.5, f32[1,1024]{1,0:T(1,128)S(1)} %bitcast.4, ...), custom_call_target="tpu_custom_call" | custom-call | tf_op jit(solution)/shard_map/pallas_call | solution.py:451
  72.7 0.0 copy-start
  72.7 1.3 copy-done
  74.1 0.0 copy-start.1
  74.1 1.3 copy-done.1
  75.4 0.0 copy-start.2
  75.4 1.3 copy-done.2
  76.7 0.0 copy-start.3
  76.7 1.4 copy-done.3
  78.0 0.0 copy-start.4
  78.0 1.4 copy-done.4
  79.4 0.0 copy-start.5
  79.4 1.3 copy-done.5
  80.7 85.7 %shard_map.74 = bf16[1024,1024]{1,0:T(8,128)(2,1)} custom-call(s32[2,7]{1,0:T(2,128)} %add_convert_fusion.valid_ref, bf16[1024,1024]{1,0:T(8,128)(2,1)} %copy-done, bf16[1024,1024]{1,0:T(8,128)(2,1)} %bitcast.6, bf16[1024,1024]{1,0:T(8,128)(2,1)} %copy-done.1, bf16[1024,1024]{1,0:T(8,128)(2,1)} %copy-done.2, f32[1,1024]{1,0:T(1,128)} %bitcast.3, ...), custom_call_target="tpu_custom_call" | custom-call | tf_op jit(solution)/shard_map/pallas_call | solution.py:498
  (1 shorter events, 0.0 us)
Async XLA Ops:
  1.4 0.7 copy-start.6
  72.7 1.3 copy-start
  74.1 1.3 copy-start.1
  75.4 1.3 copy-start.2
  76.7 1.4 copy-start.3
  78.0 1.4 copy-start.4
  79.4 1.3 copy-start.5

commit v6 on v5

--- a/solution.py
+++ b/solution.py
@@ -489,7 +489,7 @@
         ],
         axis=1,
     )
-    group = 256
+    group = 512
     ext_rows = (2 * FRAME_REACH + frame_count + keyframe_count) * frame_rows
     own_rows = frame_count * frame_rows
     whole = lambda shape: pl.BlockSpec(shape, lambda i: (0, 0), pipeline_mode=pl.Buffered(1))

time: 167 us -> 167 us (level)
  no operation moved by 1% of the time
where the time goes in v6:
time: 167 us
  Pallas kernels  156 us (93%)
  local copies, waits for them, and re-layouts  8.69 us (5%)
    pallas_call x1, Pallas kernels, fused(): pl.pallas_call(functools.partial(fused_kernel, frame_count, band_count, b...  85.9 us
    pallas_call x1, Pallas kernels, exchange(): pl.pallas_call(functools.partial(exchange_kernel, size, frame_rows), out_...  70.6 us
    unnamed x14, local copies, waits for them, and re-layouts  8.69 us

profile of v6, /device:TPU:6, one launch (start us, length us, event | category | flops | bytes accessed | tf_op | source)
XLA Modules:
  0.0 166.6 jit_solution(2927800611542804312)
XLA Ops:
  0.0 0.7 abs_compare_fusion
  0.7 0.1 compare_and_fusion
  0.8 0.6 add_convert_fusion.valid_ref
  1.4 0.0 copy-start.6
  1.4 0.7 copy-done.6
  2.1 70.6 %shard_map.73 = (bf16[1024,1024]{1,0:T(8,128)(2,1)S(1)}, bf16[1024,1024]{1,0:T(8,128)(2,1)S(1)}, bf16[1024,1024]{1,0:T(8,128)(2,1)S(1)}, bf16[1024,1024]{1,0:T(8...) custom-call(bf16[1024,1024]{1,0:T(8,128)(2,1)} %bitcast.5, f32[1,1024]{1,0:T(1,128)S(1)} %bitcast.4, ...), custom_call_target="tpu_custom_call" | custom-call | tf_op jit(solution)/shard_map/pallas_call | solution.py:451
  72.7 0.0 copy-start
  72.7 1.3 copy-done
  74.1 0.0 copy-start.1
  74.1 1.3 copy-done.1
  75.4 0.0 copy-start.2
  75.4 1.3 copy-done.2
  76.7 0.0 copy-start.3
  76.7 1.4 copy-done.3
  78.0 0.0 copy-start.4
  78.0 1.4 copy-done.4
  79.4 0.0 copy-start.5
  79.4 1.3 copy-done.5
  80.7 85.9 %shard_map.74 = bf16[1024,1024]{1,0:T(8,128)(2,1)} custom-call(s32[2,7]{1,0:T(2,128)} %add_convert_fusion.valid_ref, bf16[1024,1024]{1,0:T(8,128)(2,1)} %copy-done, bf16[1024,1024]{1,0:T(8,128)(2,1)} %bitcast.6, bf16[1024,1024]{1,0:T(8,128)(2,1)} %copy-done.1, bf16[1024,1024]{1,0:T(8,128)(2,1)} %copy-done.2, f32[1,1024]{1,0:T(1,128)} %bitcast.3, ...), custom_call_target="tpu_custom_call" | custom-call | tf_op jit(solution)/shard_map/pallas_call | solution.py:498
  (1 shorter events, 0.0 us)
Async XLA Ops:
  1.4 0.7 copy-start.6
  72.7 1.3 copy-start
  74.1 1.3 copy-start.1
  75.4 1.3 copy-start.2
  76.7 1.4 copy-start.3
  78.0 1.4 copy-start.4
  79.4 1.3 copy-start.5
